TPU v7x, 1024 devices: a whole 4x4x32 slice. The times are simulated.
1024 devices in a mesh: island: 16 (over x, y), fsdp: 64 (over z, core).
Axes of the slice: x: 4, y: 4, z: 32, core: 2. Of those that a mesh axis runs over, the one named last changes fastest.
Arguments:
- local_params: bfloat16 [16, 64, 8192, 128], P('island', None, 'fsdp'), may hold values from -450 to 450
- global_params: float32 [64, 8192, 128], P(None, 'fsdp'), may hold values from -6 to 6
- momentum: float32 [16, 6, 8192, 128], P('island', None, 'fsdp'), may hold values from -6 to 6
- owners: int32 [64, 1], replicated, may hold values from 0 to 15; in each aligned block of 64 rows (0 to 63, 64 to 127, ...) at most 6 rows name the same one
Outputs:
- new_params: float32 [64, 8192, 128], P(None, 'fsdp')
- new_momentum: float32 [16, 6, 8192, 128], P('island', None, 'fsdp')
Inputs may be any that keep to these rules, and one draw needn't show every extreme that they name: `owners`: every island owns at least one block and at most 6 blocks; some island owns exactly 6.
All inputs are finite; a program needn't handle non-finite values.
Results may differ from a plain program's by a relative error of at most 0.0028.
Values may be sent and summed in bfloat16 or wider, within the bound.
A program may use at most 64 MiB of HBM per device.

v0:
```python
import math

import jax
import jax.numpy as jnp
from jax import lax
from jax.sharding import PartitionSpec as P

ITERS = 3


decay_rate = 0.9
epsilon_norm = 1e-07
coef_a = 3.4445
coef_b = -4.775
coef_c = 2.0315


def slot_table(owner_list, islands, slots):
    onehot = (owner_list[:, None] == jnp.arange(islands, dtype=jnp.int32)[None, :]).astype(
        jnp.int32
    )
    earlier = jnp.cumsum(onehot, axis=0) - onehot
    position = jnp.sum(earlier * onehot, axis=1)
    target = owner_list * slots + position
    return (jnp.arange(islands * slots, dtype=jnp.int32)[:, None] == target[None, :]).astype(
        jnp.float32
    )


def shards(local_params, global_params, momentum, owners):
    islands = lax.axis_size("island")
    my_island = lax.axis_index("island")
    blocks, height, width = global_params.shape
    slots = momentum.shape[1]
    owner_list = owners[:, 0]
    table = slot_table(owner_list, islands, slots)
    my_table = lax.dynamic_slice_in_dim(table, my_island * slots, slots, 0)
    delta = global_params - local_params[0].astype(jnp.float32)
    per_island = blocks // islands
    summed = lax.psum_scatter(delta, "island", scatter_dimension=0, tiled=True)
    share = (summed / islands).astype(jnp.bfloat16)
    held = lax.dynamic_slice_in_dim(owner_list, my_island * per_island, per_island, 0)
    sending = held[None, :] == jnp.arange(islands, dtype=jnp.int32)[:, None]
    outgoing = jnp.where(sending[:, :, None, None], share[None], jnp.zeros_like(share)[None])
    arrived = lax.all_to_all(outgoing, "island", split_axis=0, concat_axis=0, tiled=True)
    by_block = arrived.reshape(blocks, height * width)
    pseudo = jnp.dot(my_table.astype(jnp.bfloat16), by_block, preferred_element_type=jnp.float32)
    pseudo = pseudo.reshape(slots, height, width)
    used = (jnp.sum(my_table, axis=1) > 0.5)[:, None, None]
    previous = momentum[0]
    new_momentum = jnp.where(used, decay_rate * previous + pseudo, previous)
    looking = jnp.where(used, pseudo + decay_rate * new_momentum, jnp.float32(0.0))
    squares = lax.psum(jnp.sum(looking * looking, axis=(1, 2)), "fsdp")
    iterate = looking / (jnp.sqrt(squares) + epsilon_norm)[:, None, None]
    for repeat in range(ITERS):
        partial_gram = jnp.einsum("srh,srk->shk", iterate, iterate, precision=lax.Precision.HIGHEST)
        gram = lax.psum(partial_gram, "fsdp")
        poly = coef_b * gram + coef_c * jnp.einsum(
            "shk,skj->shj", gram, gram, precision=lax.Precision.HIGHEST
        )
        iterate = coef_a * iterate + jnp.einsum(
            "srh,shk->srk", iterate, poly, precision=lax.Precision.HIGHEST
        )
    everyone = lax.all_gather(iterate, "island", axis=0, tiled=True)
    update = jnp.dot(
        table.T, everyone.reshape(islands * slots, height * width), precision=lax.Precision.HIGHEST
    )
    factor = math.sqrt(height * lax.axis_size("fsdp") / width)
    new_params = global_params - factor * update.reshape(blocks, height, width)
    return (new_params, new_momentum[None])


def solution(mesh):
    in_specs = (
        P("island", None, "fsdp", None),
        P(None, "fsdp", None),
        P("island", None, "fsdp", None),
        P(),
    )
    out_specs = (P(None, "fsdp", None), P("island", None, "fsdp", None))
    return jax.shard_map(shards, mesh=mesh, in_specs=in_specs, out_specs=out_specs, check_vma=False)
```

profile of v0, /device:TPU:1, one launch (start us, length us, event | category | flops | bytes accessed | tf_op | source)
XLA Modules:
  0.0 1566.7 jit_solution(3034603947019618371)
XLA Ops:
  7.2 5.8 convert_subtract_fusion
  13.0 0.6 copy-done.1
  13.6 0.1 dynamic-slice_bitcast_fusion
  13.7 120.5 %reduce-scatter.2.cloned.1.call-done = f32[4,128,128]{2,1,0:T(8,128)} async-done(((f32[64,128,128]{2,1,0:T(8,128)}), f32[4,128,128]{2,1,0:T(8,128)}) %reduce-scatter.2.cloned.1.call-update) | async-done | bytes 262160 | tf_op jit(solution)/shard_map/reduce_scatter | solution.py:40
  134.2 1.0 multiply_convert_fusion
  135.1 1.5 broadcast_select_fusion
  136.7 4.8 all-to-all-start
  141.5 0.0 all-reduce.4.cloned.1.call-start
  141.6 0.1 fusion.15
  141.6 0.1 reduce_window_sum.11
  141.7 0.2 select_reduce_fusion
  141.9 0.1 convert_reduce_fusion
  142.1 24.7 %all-to-all-done = bf16[16,4,128,128]{3,2,1,0:T(8,128)(2,1)S(1)} async-done(((bf16[16,4,128,128]{3,2,1,0:T(8,128)(2,1)}), bf16[16,4,128,128]{3,2,1,0:T(8,128)(2,1)S(1)}, u32[]{:S(2)}, u32[]{:S(2)}) %all-to-all-start) | async-done | bytes 2097184 | tf_op jit(solution)/shard_map/all_to_all | solution.py:45
  166.8 1.2 fusion.5
  168.0 0.9 multiply_reduce_fusion
  169.0 97.7 %psum.28 = f32[6]{0:T(128)S(1)} all-reduce(f32[6]{0:T(128)S(1)} %get-tuple-element.10), channel_id=1, replica_groups=mesh['island'=16,'fsdp'=64] {'fsdp'}, use_global_device_ids=true, to_apply=%region_5.6 | all-reduce | flops 6 | bytes 48 | tf_op jit(solution)/shard_map/psum | solution.py:53
  266.7 1.6 fusion.13
  268.4 391.3 %all-reduce.4.cloned.1.call-done = f32[6,128,128]{2,1,0:T(8,128)} async-done(((f32[6,128,128]{2,1,0:T(8,128)}), f32[6,128,128]{2,1,0:T(8,128)}) %all-reduce.4.cloned.1.call-update) | async-done | bytes 393232 | tf_op jit(solution)/shard_map/psum | solution.py:57
  659.7 1.8 fusion.10
  661.5 0.6 convolution_add_fusion.2
  662.1 1.6 fusion.19
  663.7 389.5 %all-reduce.6.cloned.1.call-done = f32[6,128,128]{2,1,0:T(8,128)} async-done(((f32[6,128,128]{2,1,0:T(8,128)}), f32[6,128,128]{2,1,0:T(8,128)}) %all-reduce.6.cloned.1.call-update) | async-done | bytes 393232 | tf_op jit(solution)/shard_map/psum | solution.py:57
  1053.3 1.8 fusion.9
  1055.1 0.6 convolution_add_fusion.1
  1055.6 1.6 fusion.20
  1057.2 0.2 all-gather.2.cloned.1.call-start
  1057.4 389.3 %all-reduce.8.cloned.1.call-done = f32[6,128,128]{2,1,0:T(8,128)} async-done(((f32[6,128,128]{2,1,0:T(8,128)}), f32[6,128,128]{2,1,0:T(8,128)}) %all-reduce.8.cloned.1.call-update) | async-done | bytes 393232 | tf_op jit(solution)/shard_map/psum | solution.py:57
  1446.8 1.8 fusion.8
  1448.6 1.3 convolution_add_fusion
  1449.9 92.8 %all-gather.2.cloned.1.call-done = f32[96,128,128]{2,1,0:T(8,128)} async-done(((f32[6,128,128]{2,1,0:T(8,128)}), f32[96,128,128]{2,1,0:T(8,128)}) %all-gather.2.cloned.1.call-update) | async-done | bytes 6291472 | tf_op jit(solution)/shard_map/all_gather | solution.py:64
  1542.7 13.0 copy_subtract_fusion
  1555.7 4.4 copy.72
  (16 shorter events, 0.3 us)
Async XLA Ops:
  7.2 127.0 %reduce-scatter.2.cloned.1.call-start = ((), (), s32[]{:S(2)}) async-start(), calls=%async_computation.2 | async-start | bytes 4456448 | tf_op jit(solution)/shard_map/reduce_scatter | solution.py:40
  13.0 0.7 copy-start.1
  136.7 31.4 %copy-start = (f32[1,6,128,128]{3,2,1,0:T(8,128)S(1)}, f32[1,6,128,128]{3,2,1,0:T(8,128)}, u32[]{:S(2)}) copy-start(f32[1,6,128,128]{3,2,1,0:T(8,128)} %param.6) | copy-start | bytes 1179652
  136.7 30.1 %all-to-all-start = ((bf16[16,4,128,128]{3,2,1,0:T(8,128)(2,1)}), bf16[16,4,128,128]{3,2,1,0:T(8,128)(2,1)S(1)}, u32[]{:S(2)}, u32[]{:S(2)}) async-start(bf16[16,4,128,128]{3,2,1,0:T(8,128)(2,1)} %broadcast_select_fusion), calls=%async_computation.1 | async-start | bytes 4194304 | tf_op jit(solution)/shard_map/all_to_all | solution.py:45
  141.5 518.2 %all-reduce.4.cloned.1.call-start = ((), (), s32[]{:S(2)}) async-start(), calls=%async_computation.3 | async-start | bytes 786432 | tf_op jit(solution)/shard_map/psum | solution.py:57
  268.3 784.9 %all-reduce.6.cloned.1.call-start = ((), (), s32[]{:S(2)}) async-start(), calls=%async_computation.4 | async-start | bytes 786432 | tf_op jit(solution)/shard_map/psum | solution.py:57
  663.7 783.1 %all-reduce.8.cloned.1.call-start = ((), (), s32[]{:S(2)}) async-start(), calls=%async_computation.5 | async-start | bytes 786432 | tf_op jit(solution)/shard_map/psum | solution.py:57
  1057.2 485.5 %all-gather.2.cloned.1.call-start = ((), (), s32[]{:S(2)}) async-start(), calls=%async_computation.6 | async-start | bytes 6684672 | tf_op jit(solution)/shard_map/all_gather | solution.py:64
Sparse Core Ops, SparseCore 0:
  13.9 120.1 reduce-scatter.1
  268.4 391.2 all-reduce.3
  663.8 389.4 all-reduce.5
  1057.3 389.4 all-reduce.7
  1451.4 91.2 all-gather.1
where the time goes:
time: 1570 us
  waiting for transfers between devices  1410 us (90%)
  blocking collectives  97.7 us (6%)
  matrix products  26.8 us (2%)
    psum x3, waiting for transfers between devices, shards(): gram = lax.psum(partial_gram, 'fsdp')  1170 us
    reduce_scatter x1, waiting for transfers between devices, shards(): summed = lax.psum_scatter(delta, 'island', scatter_dimension=0, tiled=True)  120 us
    psum x1, blocking collectives, shards(): squares = lax.psum(jnp.sum(looking * looking, axis=(1, 2)), 'fsdp')  97.7 us
    all_gather x1, waiting for transfers between devices, shards(): everyone = lax.all_gather(iterate, 'island', axis=0, tiled=True)  92.8 us
  transfers between devices with their start and end apart: 6, of which 6 were waited for; matrix products, arithmetic and copies ran while one was open for 0% of the time, Pallas kernels for 0%

commit v1 on v0

v1 whole, which is shorter than its diff:
```python
import math

import jax
import jax.numpy as jnp
from jax import lax
from jax.experimental import pallas as pl
from jax.experimental.pallas import tpu as pltpu
from jax.sharding import PartitionSpec as P

MESH = pl.DeviceIdType.MESH
HIGHEST = lax.Precision.HIGHEST
decay_rate = 0.9
epsilon_norm = 1e-07
coef_a = 3.4445
coef_b = -4.775
coef_c = 2.0315

N = 4
NEAR = 4
FAR = 8
HALF = 64
LOOK_P = 1.0 + decay_rate
LOOK_M = decay_rate * decay_rate


def kernel(
    table, local, globe, mom, xall, newmom,
    lown, g_a, g_b, r1a, r1b, s2a, s2b, r2a, r2b, look, lookall, gpart, gsend, rnear, fown, rfar, gfull,
    load_sem, g_sem, s1_send, s1_recv, s2_send, s2_recv,
    l_send, l_recv, lf_send, lf_recv, x_send, x_recv, xf_send, xf_recv, n_send, n_recv, f_send, f_recv, a_send, a_recv,
):
    island, fsdp = lax.axis_index("island"), lax.axis_index("fsdp")
    x, y = island // N, island % N
    z, core = fsdp // 2, fsdp % 2
    near = (z % NEAR) * 2 + core

    def at_xy(px, py):
        return (px * N + py, fsdp)

    def x_peer(j):
        return at_xy((x + j) % N, y)

    def y_peer(j):
        return at_xy(x, (y + j) % N)

    def near_peer(q):
        other = (near + q) % (2 * NEAR)
        return (island, ((z // NEAR) * NEAR + other // 2) * 2 + other % 2)

    def far_peer(q):
        return (island, ((z + NEAR * q) % (NEAR * FAR)) * 2 + core)

    barrier = pltpu.get_barrier_semaphore()
    peers = [x_peer(j) for j in range(1, N)] + [y_peer(j) for j in range(1, N)]
    peers += [near_peer(q) for q in range(1, 2 * NEAR)] + [far_peer(q) for q in range(1, FAR)]
    for peer in peers:
        pl.semaphore_signal(barrier, inc=1, device_id=peer, device_id_type=MESH)

    order = [(t, j) for t in (1, 2, 3, 0) for j in (1, 2, 3, 0)]
    loads = {}
    for t, j in order:
        place = ((x + t) % N, (y + j) % N)
        loads[t, j] = pltpu.make_async_copy(local.at[place], lown.at[place], load_sem.at[t * N + j])
        loads[t, j].start()
    load_a = pltpu.make_async_copy(globe.at[:, y, :, 0:HALF, :], g_a, g_sem.at[0])
    load_b = pltpu.make_async_copy(globe.at[x, :, :, HALF : 2 * HALF, :], g_b, g_sem.at[1])
    load_a.start()
    load_b.start()
    pl.semaphore_wait(barrier, len(peers))

    def remote(src, dst, send, recv, peer):
        return pltpu.make_async_remote_copy(
            src_ref=src, dst_ref=dst, send_sem=send, recv_sem=recv, device_id=peer, device_id_type=MESH
        )

    sent = []
    first_a, first_b = {}, {}
    inject = 16.0 * LOOK_M / LOOK_P
    for t, j in order:
        px, py = (x + t) % N, (y + j) % N
        loads[t, j].wait()

        def put(k, _, px=px, py=py):
            block = (px * N + py) * N + k
            scale = table[64 + block].astype(jnp.float32) * inject
            term = lown[px, py, k].astype(jnp.float32) - scale * mom[table[block]]
            lown[px, py, k] = term.astype(jnp.bfloat16)
            return 0

        lax.fori_loop(0, N, put, 0)
        if j:
            at = (j - 1) * N + t
            copy = remote(
                lown.at[px, py, :, 0:HALF, :], r1a.at[j - 1, px], s1_send.at[0, at], s1_recv.at[0, at], y_peer(j)
            )
            copy.start()
            first_a[t, j] = copy
        if t:
            at = (t - 1) * N + j
            copy = remote(
                lown.at[px, py, :, HALF : 2 * HALF, :], r1b.at[t - 1, py], s1_send.at[1, at], s1_recv.at[1, at], x_peer(t)
            )
            copy.start()
            first_b[t, j] = copy
    sent += list(first_a.values()) + list(first_b.values())
    load_a.wait()
    load_b.wait()

    def line_a(t):
        px = (x + t) % N
        for j in range(1, N):
            first_a[t, j].wait_recv()
        total = lown[px, y, :, 0:HALF, :].astype(jnp.float32)
        for j in range(1, N):
            total = total + r1a[j - 1, px].astype(jnp.float32)
        return N * g_a[px] - total

    def line_b(j):
        py = (y + j) % N
        for t in range(1, N):
            first_b[t, j].wait_recv()
        total = lown[x, py, :, HALF : 2 * HALF, :].astype(jnp.float32)
        for t in range(1, N):
            total = total + r1b[t - 1, py].astype(jnp.float32)
        return N * g_b[py] - total

    second = []
    for s in range(1, N):
        s2a[s - 1] = line_a(s).astype(jnp.bfloat16)
        copy_a = remote(s2a.at[s - 1], r2a.at[s - 1], s2_send.at[0, s - 1], s2_recv.at[0, s - 1], x_peer(s))
        copy_a.start()
        s2b[s - 1] = line_b(s).astype(jnp.bfloat16)
        copy_b = remote(s2b.at[s - 1], r2b.at[s - 1], s2_send.at[1, s - 1], s2_recv.at[1, s - 1], y_peer(s))
        copy_b.start()
        second += [copy_a, copy_b]
    look[:, 0:HALF, :] = line_a(0)
    look[:, HALF : 2 * HALF, :] = line_b(0)
    for copy in second:
        copy.wait_recv()
    sent += second
    total_a, total_b = look[:, 0:HALF, :], look[:, HALF : 2 * HALF, :]
    for s in range(N - 1):
        total_a = total_a + r2a[s].astype(jnp.float32)
        total_b = total_b + r2b[s].astype(jnp.float32)
    look[:, 0:HALF, :] = total_a * (LOOK_P / 16.0)
    look[:, HALF : 2 * HALF, :] = total_b * (LOOK_P / 16.0)
    lookall[x, y] = look[...].astype(jnp.bfloat16)

    def gather_own(buf, send, recv):
        copies = []
        for j in range(1, N):
            for way, peer in enumerate((x_peer(j), y_peer(j))):
                copy = remote(buf.at[x, y], buf.at[x, y], send.at[way, j - 1], recv.at[way, j - 1], peer)
                copy.start()
                copies.append(copy)
        return copies

    def gather_forward(buf, direct, send, recv):
        copies = []
        for j in range(1, N):
            for way in range(2):
                direct[(j - 1) * 2 + way].wait_recv()
                for i in range(1, N):
                    at = (j - 1) * (N - 1) + i - 1
                    if way == 0:
                        piece = buf.at[(x - j + N) % N, y, :, 0:HALF, :]
                        copy = remote(piece, piece, send.at[0, at], recv.at[0, at], y_peer(i))
                    else:
                        piece = buf.at[x, (y - j + N) % N, :, HALF : 2 * HALF, :]
                        copy = remote(piece, piece, send.at[1, at], recv.at[1, at], x_peer(i))
                    copy.start()
                    copies.append(copy)
        return copies

    look_direct = gather_own(lookall, l_send, l_recv)
    sent += look_direct

    for k in range(N):
        block = look[k]
        gram = lax.dot_general(
            block, block, (((0,), (0,)), ((), ())), precision=HIGHEST, preferred_element_type=jnp.float32
        )
        gpart[2 * k] = gram[0:HALF]
        gpart[2 * k + 1] = gram[HALF : 2 * HALF]
    gsend[...] = gpart[...].astype(jnp.bfloat16)
    steps = []
    for q in range(1, 2 * NEAR):
        other = (near + q) % (2 * NEAR)
        copy = remote(gsend.at[other], rnear.at[q - 1], n_send.at[q - 1], n_recv.at[q - 1], near_peer(q))
        copy.start()
        steps.append(copy)
    for copy in steps:
        copy.wait_recv()
    sent += steps
    mine = gpart[near]
    for q in range(2 * NEAR - 1):
        mine = mine + rnear[q].astype(jnp.float32)
    fown[...] = mine.astype(jnp.bfloat16)
    steps = []
    for q in range(1, FAR):
        copy = remote(fown, rfar.at[q - 1], f_send.at[q - 1], f_recv.at[q - 1], far_peer(q))
        copy.start()
        steps.append(copy)
    look_forward = gather_forward(lookall, look_direct, lf_send, lf_recv)
    sent += look_forward
    for copy in steps:
        copy.wait_recv()
    sent += steps
    for q in range(FAR - 1):
        mine = mine + rfar[q].astype(jnp.float32)
    gfull[near] = mine.astype(jnp.bfloat16)
    steps = []
    for q in range(1, 2 * NEAR):
        copy = remote(gfull.at[near], gfull.at[near], a_send.at[q - 1], a_recv.at[q - 1], near_peer(q))
        copy.start()
        steps.append(copy)
    for copy in steps:
        copy.wait_recv()
    sent += steps

    def mm(left, right):
        return jnp.dot(left, right, precision=HIGHEST, preferred_element_type=jnp.float32)

    rows = lax.broadcasted_iota(jnp.int32, (2 * HALF, 2 * HALF), 0)
    cols = lax.broadcasted_iota(jnp.int32, (2 * HALF, 2 * HALF), 1)
    eye = jnp.where(rows == cols, 1.0, 0.0).astype(jnp.float32)
    grams, scales = [], []
    for k in range(N):
        gram = gfull[2 * k : 2 * k + 2].astype(jnp.float32).reshape(2 * HALF, 2 * HALF)
        squares = jnp.sum(jnp.sum(gram * eye, axis=1, keepdims=True), axis=0, keepdims=True)
        scale = 1.0 / (jnp.sqrt(squares) + epsilon_norm)
        grams.append(gram * scale * scale)
        scales.append(scale)
    mults = None
    for step in range(3):
        squared = [mm(gram, gram) for gram in grams]
        polys = [coef_a * eye + coef_b * gram + coef_c * square for gram, square in zip(grams, squared)]
        if step < 2:
            inner = [mm(poly, gram) for poly, gram in zip(polys, grams)]
            grams = [mm(poly, part) for poly, part in zip(polys, inner)]
        mults = polys if mults is None else [mm(mult, poly) for mult, poly in zip(mults, polys)]
    for k in range(N):
        xall[x, y, k] = mm(look[k], mults[k] * scales[k]).astype(jnp.bfloat16)

    x_direct = gather_own(xall, x_send, x_recv)
    sent += x_direct

    for copy in look_forward:
        copy.wait_recv()

    for s in range(newmom.shape[0]):
        block = table[128 + s]
        used = table[136 + s]
        old = mom[s]
        seen = lookall[block // 16, (block // N) % N, block % N].astype(jnp.float32)
        fresh = decay_rate * old + (seen - LOOK_M * old) * (1.0 / LOOK_P)
        newmom[s] = jnp.where(used > 0, fresh, old)

    x_forward = gather_forward(xall, x_direct, xf_send, xf_recv)
    sent += x_forward
    for copy in x_forward:
        copy.wait_recv()
    for copy in sent:
        copy.wait_send()


def shards(local_params, global_params, momentum, owners):
    my_island = lax.axis_index("island")
    blocks, height, width = global_params.shape
    slots = momentum.shape[1]
    owner = owners[:, 0]
    ids = jnp.arange(blocks, dtype=jnp.int32)
    earlier = (owner[None, :] == owner[:, None]) & (ids[None, :] < ids[:, None])
    position = jnp.sum(earlier.astype(jnp.int32), axis=1)
    own = owner == my_island
    route = jnp.where(own, position, 0)
    hit = own[None, :] & (position[None, :] == jnp.arange(8, dtype=jnp.int32)[:, None])
    holds = jnp.sum(jnp.where(hit, ids[None, :], 0), axis=1)
    used = jnp.sum(hit.astype(jnp.int32), axis=1)
    table = jnp.concatenate([route, own.astype(jnp.int32), holds, used])

    bf, f4 = jnp.bfloat16, jnp.float32
    dma = pltpu.SemaphoreType.DMA
    vmem = pltpu.VMEM
    gathered, new_momentum = pl.pallas_call(
        kernel,
        out_shape=(
            jax.ShapeDtypeStruct((N, N, N, height, width), bf),
            jax.ShapeDtypeStruct((slots, height, width), f4),
        ),
        in_specs=[
            pl.BlockSpec(memory_space=pltpu.SMEM),
            pl.BlockSpec(memory_space=pl.ANY),
            pl.BlockSpec(memory_space=pl.ANY),
            pl.BlockSpec(memory_space=vmem),
        ],
        out_specs=(pl.BlockSpec(memory_space=vmem), pl.BlockSpec(memory_space=vmem)),
        scratch_shapes=[
            vmem((N, N, N, height, width), bf),
            vmem((N, N, HALF, width), f4),
            vmem((N, N, HALF, width), f4),
            vmem((N - 1, N, N, HALF, width), bf),
            vmem((N - 1, N, N, HALF, width), bf),
            vmem((N - 1, N, HALF, width), bf),
            vmem((N - 1, N, HALF, width), bf),
            vmem((N - 1, N, HALF, width), bf),
            vmem((N - 1, N, HALF, width), bf),
            vmem((N, height, width), f4),
            vmem((N, N, N, height, width), bf),
            vmem((2 * N, HALF, width), f4),
            vmem((2 * N, HALF, width), bf),
            vmem((2 * NEAR - 1, HALF, width), bf),
            vmem((HALF, width), bf),
            vmem((FAR - 1, HALF, width), bf),
            vmem((2 * N, HALF, width), bf),
            dma((N * N,)),
            dma((2,)),
            dma((2, (N - 1) * N)),
            dma((2, (N - 1) * N)),
            dma((2, N - 1)),
            dma((2, N - 1)),
            dma((2, N - 1)),
            dma((2, N - 1)),
            dma((2, (N - 1) * (N - 1))),
            dma((2, (N - 1) * (N - 1))),
            dma((2, N - 1)),
            dma((2, N - 1)),
            dma((2, (N - 1) * (N - 1))),
            dma((2, (N - 1) * (N - 1))),
            dma((2 * NEAR - 1,)),
            dma((2 * NEAR - 1,)),
            dma((FAR - 1,)),
            dma((FAR - 1,)),
            dma((2 * NEAR - 1,)),
            dma((2 * NEAR - 1,)),
        ],
        compiler_params=pltpu.CompilerParams(
            collective_id=0, has_side_effects=True, vmem_limit_bytes=32 * 1024 * 1024
        ),
        name="outer_step",
    )(
        table,
        local_params.reshape(N, N, N, height, width),
        global_params.reshape(N, N, N, height, width),
        momentum[0],
    )
    factor = math.sqrt(height * lax.axis_size("fsdp") / width)
    update = gathered.reshape(blocks, height, width).astype(f4)
    return (global_params - factor * update, new_momentum[None])


def solution(mesh):
    in_specs = (
        P("island", None, "fsdp", None),
        P(None, "fsdp", None),
        P("island", None, "fsdp", None),
        P(),
    )
    out_specs = (P(None, "fsdp", None), P("island", None, "fsdp", None))
    return jax.shard_map(shards, mesh=mesh, in_specs=in_specs, out_specs=out_specs, check_vma=False)
```

time: 1570 us -> 106 us (0.07)
  waiting for transfers between devices: 1410 us -> 0 us
  blocking collectives: 97.7 us -> 0 us
  Pallas kernels: 0 us -> 93.9 us
  matrix products: 26.8 us -> 0 us
    psum x3 -> x0, waiting for transfers between devices: 1170 us -> none  [shards(): gram = lax.psum(partial_gram, 'fsdp')]
    reduce_scatter x1 -> x0, waiting for transfers between devices: 120 us -> none  [shards(): summed = lax.psum_scatter(delta, 'island', scatter_dimension=0, tiled=True)]
    psum x1 -> x0, blocking collectives: 97.7 us -> none  [shards(): squares = lax.psum(jnp.sum(looking * looking, axis=(1, 2)), 'fsdp')]
    pallas_call x0 -> x1, Pallas kernels: none -> 93.9 us  [shards(): pl.pallas_call(kernel, out_shape=(jax.ShapeDtypeStruct((N, N, N, height,...]
    all_gather x1 -> x0, waiting for transfers between devices: 92.8 us -> none  [shards(): everyone = lax.all_gather(iterate, 'island', axis=0, tiled=True)]
    dot_general x11 -> x0, matrix products: 26.8 us -> none  [the longest x1 13 us: shards(): jnp.dot(table.T, everyone.reshape(islands * slots, height * width), preci...]
    all_to_all x1 -> x0, waiting for transfers between devices: 24.7 us -> none  [shards(): lax.all_to_all(outgoing, 'island', split_axis=0, concat_axis=0, tiled=True)]
  transfers between devices with their start and end apart: 6 -> 0, of which waited for: 6 -> 0; matrix products, arithmetic and copies ran while one was open for 0% -> 0% of each run, Pallas kernels for 0% -> 0%
where the time goes in v1:
time: 106 us; the launch traced here: 105 us
  Pallas kernels  93.9 us (89%)
  local copies, waits for them, and re-layouts  5.53 us (5%)
  other arithmetic  5.19 us (5%)
    pallas_call x1, Pallas kernels, shards(): pl.pallas_call(kernel, out_shape=(jax.ShapeDtypeStruct((N, N, N, height,...  93.9 us
    unnamed x7, local copies, waits for them, and re-layouts  5.53 us
    sub x1, other arithmetic, shards(): return (global_params - factor * update, new_momentum[None])  2.84 us

profile of v1, /device:TPU:1, one launch (start us, length us, event | category | flops | bytes accessed | tf_op | source)
XLA Modules:
  0.0 105.3 jit_solution(12014641617684963510)
XLA Ops:
  0.6 0.9 convert_reduce_fusion
  1.5 0.7 broadcast_select_fusion
  2.2 0.1 select_reduce_fusion
  2.4 0.1 pad_add_fusion.table
  2.4 0.0 copy-start
  2.4 2.2 %copy-done = f32[64,128,128]{2,1,0:T(8,128)S(1)} copy-done((f32[64,128,128]{2,1,0:T(8,128)S(1)}, f32[64,128,128]{2,1,0:T(8,128)}, u32[]{:S(2)}) %copy-start) | copy-done | bytes 4194328
  4.6 0.0 copy-start.1
  4.6 1.6 %copy-done.1 = bf16[1,64,128,128]{3,2,1,0:T(8,128)(2,1)S(1)} copy-done((bf16[1,64,128,128]{3,2,1,0:T(8,128)(2,1)S(1)}, bf16[1,64,128,128]{3,2,1,0:T(8,128)(2,1)}, u32[]{:S(2)}) %copy-start.1) | copy-done | bytes 2097176
  6.2 0.0 copy-start.2
  6.2 1.0 copy-done.2
  7.2 93.9 %outer_step.1 = (bf16[4,4,4,128,128]{4,3,2,1,0:T(8,128)(2,1)S(1)}, f32[6,128,128]{2,1,0:T(8,128)S(1)}) custom-call(s32[144]{0:T(256)S(1)} %pad_add_fusion.table, bf16[4,4,4,128,128]{4,3,2,1,0:T(8,128)(2,1)S(1)} %bitcast.10, f32[4,4,4,128,128]{4,3,2,1,0:T(8,128)S(1)} %bitcast.9, f32[6,128,128]{2,1,0:T(8,128)S(1)} %bitcast.11), custom_call_target="tpu_custom_call" | custom-call | tf_op jit(solution)/shard_map/outer_step/pallas_call | solution.py:285
  101.1 0.5 convert_multiply_fusion
  101.7 2.8 %bitcast_subtract_fusion = f32[64,128,128]{2,1,0:T(8,128)} fusion(f32[64,128,128]{2,1,0:T(8,128)S(1)} %copy-done, f32[4,4,4,128,128]{4,3,2,1,0:T(8,128)S(1)} %convert_multiply_fusion), kind=kLoop, calls=%fused_computation | loop fusion | flops 1048576 | bytes 12582912 | tf_op jit(solution)/shard_map/sub | solution.py:349
  104.5 0.7 copy.7
  (1 shorter events, 0.0 us)
Async XLA Ops:
  2.4 2.2 %copy-start = (f32[64,128,128]{2,1,0:T(8,128)S(1)}, f32[64,128,128]{2,1,0:T(8,128)}, u32[]{:S(2)}) copy-start(f32[64,128,128]{2,1,0:T(8,128)} %param.5) | copy-start | bytes 12582916
  4.6 1.6 %copy-start.1 = (bf16[1,64,128,128]{3,2,1,0:T(8,128)(2,1)S(1)}, bf16[1,64,128,128]{3,2,1,0:T(8,128)(2,1)}, u32[]{:S(2)}) copy-start(bf16[1,64,128,128]{3,2,1,0:T(8,128)(2,1)} %param.4) | copy-start | bytes 6291460
  6.2 1.0 copy-start.2

commit v2 on v1

--- a/solution.py
+++ b/solution.py
@@ -52,7 +52,7 @@
 
     barrier = pltpu.get_barrier_semaphore()
     peers = [x_peer(j) for j in range(1, N)] + [y_peer(j) for j in range(1, N)]
-    peers += [near_peer(q) for q in range(1, 2 * NEAR)] + [far_peer(q) for q in range(1, FAR)]
+    peers += [near_peer(q) for q in range(1, 2 * NEAR)] + [far_peer(q) for q in (1, 2, FAR - 2, FAR - 1)]
     for peer in peers:
         pl.semaphore_signal(barrier, inc=1, device_id=peer, device_id_type=MESH)
 
@@ -197,13 +197,22 @@
         mine = mine + rnear[q].astype(jnp.float32)
     fown[...] = mine.astype(jnp.bfloat16)
     steps = []
-    for q in range(1, FAR):
-        copy = remote(fown, rfar.at[q - 1], f_send.at[q - 1], f_recv.at[q - 1], far_peer(q))
+    for slot, q in enumerate((2, FAR - 2, 1, FAR - 1)):
+        copy = remote(fown, rfar.at[slot], f_send.at[slot], f_recv.at[slot], far_peer(q))
         copy.start()
         steps.append(copy)
+    steps[0].wait_recv()
+    for slot, q in ((4, 2), (5, 1)):
+        copy = remote(rfar.at[0], rfar.at[slot], f_send.at[slot], f_recv.at[slot], far_peer(q))
+        copy.start()
+        steps.append(copy)
+    steps[1].wait_recv()
+    copy = remote(rfar.at[1], rfar.at[6], f_send.at[6], f_recv.at[6], far_peer(FAR - 1))
+    copy.start()
+    steps.append(copy)
     look_forward = gather_forward(lookall, look_direct, lf_send, lf_recv)
     sent += look_forward
-    for copy in steps:
+    for copy in steps[2:]:
         copy.wait_recv()
     sent += steps
     for q in range(FAR - 1):
@@ -278,6 +287,9 @@
     holds = jnp.sum(jnp.where(hit, ids[None, :], 0), axis=1)
     used = jnp.sum(hit.astype(jnp.int32), axis=1)
     table = jnp.concatenate([route, own.astype(jnp.int32), holds, used])
+
+    def in_hbm(array):
+        return pltpu.with_memory_space_constraint(array, pltpu.HBM)
 
     bf, f4 = jnp.bfloat16, jnp.float32
     dma = pltpu.SemaphoreType.DMA
@@ -340,8 +352,8 @@
         name="outer_step",
     )(
         table,
-        local_params.reshape(N, N, N, height, width),
-        global_params.reshape(N, N, N, height, width),
+        in_hbm(local_params.reshape(N, N, N, height, width)),
+        in_hbm(global_params.reshape(N, N, N, height, width)),
         momentum[0],
     )
     factor = math.sqrt(height * lax.axis_size("fsdp") / width)

time: 106 us -> 98.3 us (0.927)
  Pallas kernels: 93.9 us -> 88.9 us
  local copies, waits for them, and re-layouts: 5.53 us -> 3.38 us
    pallas_call x1, Pallas kernels: 93.9 us -> 88.9 us  [shards(): pl.pallas_call(kernel, out_shape=(jax.ShapeDtypeStruct((N, N, N, height,...]
    unnamed x7 -> x5, local copies, waits for them, and re-layouts: 5.53 us -> 3.38 us
where the time goes in v2:
time: 98.3 us; the launch traced here: 98.1 us
  Pallas kernels  88.9 us (90%)
  other arithmetic  5.18 us (5%)
  local copies, waits for them, and re-layouts  3.38 us (3%)
    pallas_call x1, Pallas kernels, shards(): pl.pallas_call(kernel, out_shape=(jax.ShapeDtypeStruct((N, N, N, height,...  88.9 us
    unnamed x5, local copies, waits for them, and re-layouts  3.38 us
    sub x1, other arithmetic, shards(): return (global_params - factor * update, new_momentum[None])  2.83 us

profile of v2, /device:TPU:1, one launch (start us, length us, event | category | flops | bytes accessed | tf_op | source)
XLA Modules:
  0.0 98.1 jit_solution(226941810153029422)
XLA Ops:
  0.6 0.9 convert_reduce_fusion
  1.5 0.7 broadcast_select_fusion
  2.2 0.1 select_reduce_fusion
  2.4 0.1 pad_add_fusion.table
  2.4 0.0 copy-start
  2.4 1.0 %copy-done = f32[1,6,128,128]{3,2,1,0:T(8,128)S(1)} copy-done((f32[1,6,128,128]{3,2,1,0:T(8,128)S(1)}, f32[1,6,128,128]{3,2,1,0:T(8,128)}, u32[]{:S(2)}) %copy-start) | copy-done | bytes 393240
  3.5 88.9 %outer_step.1 = (bf16[4,4,4,128,128]{4,3,2,1,0:T(8,128)(2,1)S(1)}, f32[6,128,128]{2,1,0:T(8,128)S(1)}) custom-call(s32[144]{0:T(256)S(1)} %pad_add_fusion.table, bf16[4,4,4,128,128]{4,3,2,1,0:T(8,128)(2,1)} %bitcast.12, f32[4,4,4,128,128]{4,3,2,1,0:T(8,128)} %bitcast.11, f32[6,128,128]{2,1,0:T(8,128)S(1)} %bitcast.9), custom_call_target="tpu_custom_call" | custom-call | tf_op jit(solution)/shard_map/outer_step/pallas_call | solution.py:297
  92.3 0.0 copy-start.1
  92.3 0.5 convert_multiply_fusion
  92.9 1.6 %copy-done.1 = f32[64,128,128]{2,1,0:T(8,128)S(1)} copy-done((f32[64,128,128]{2,1,0:T(8,128)S(1)}, f32[64,128,128]{2,1,0:T(8,128)}, u32[]{:S(2)}) %copy-start.1) | copy-done | bytes 4194328
  94.5 2.8 %bitcast_subtract_fusion = f32[64,128,128]{2,1,0:T(8,128)} fusion(f32[64,128,128]{2,1,0:T(8,128)S(1)} %copy-done.1, f32[4,4,4,128,128]{4,3,2,1,0:T(8,128)S(1)} %convert_multiply_fusion), kind=kLoop, calls=%fused_computation | loop fusion | flops 1048576 | bytes 12582912 | tf_op jit(solution)/shard_map/sub | solution.py:361
  97.4 0.7 copy.7
  (1 shorter events, 0.0 us)
Async XLA Ops:
  2.4 1.0 %copy-start = (f32[1,6,128,128]{3,2,1,0:T(8,128)S(1)}, f32[1,6,128,128]{3,2,1,0:T(8,128)}, u32[]{:S(2)}) copy-start(f32[1,6,128,128]{3,2,1,0:T(8,128)} %param.6) | copy-start | bytes 1179652
  92.3 2.2 %copy-start.1 = (f32[64,128,128]{2,1,0:T(8,128)S(1)}, f32[64,128,128]{2,1,0:T(8,128)}, u32[]{:S(2)}) copy-start(f32[64,128,128]{2,1,0:T(8,128)} %param.5) | copy-start | bytes 12582916

commit v3 on v2

--- a/solution.py
+++ b/solution.py
@@ -1,3 +1,4 @@
+import functools
 import math
 
 import jax
@@ -24,8 +25,8 @@
 
 
 def kernel(
-    table, local, globe, mom, xall, newmom,
-    lown, g_a, g_b, r1a, r1b, s2a, s2b, r2a, r2b, look, lookall, gpart, gsend, rnear, fown, rfar, gfull,
+    factor, table, local, globe, mom, newp, newmom,
+    lown, xall, r1a, r1b, s2a, s2b, r2a, r2b, look, lookall, gpart, gsend, rnear, fown, rfar, gfull,
     load_sem, g_sem, s1_send, s1_recv, s2_send, s2_recv,
     l_send, l_recv, lf_send, lf_recv, x_send, x_recv, xf_send, xf_recv, n_send, n_recv, f_send, f_recv, a_send, a_recv,
 ):
@@ -62,11 +63,8 @@
         place = ((x + t) % N, (y + j) % N)
         loads[t, j] = pltpu.make_async_copy(local.at[place], lown.at[place], load_sem.at[t * N + j])
         loads[t, j].start()
-    load_a = pltpu.make_async_copy(globe.at[:, y, :, 0:HALF, :], g_a, g_sem.at[0])
-    load_b = pltpu.make_async_copy(globe.at[x, :, :, HALF : 2 * HALF, :], g_b, g_sem.at[1])
-    load_a.start()
-    load_b.start()
-    pl.semaphore_wait(barrier, len(peers))
+    load_g = pltpu.make_async_copy(globe, newp, g_sem)
+    load_g.start()
 
     def remote(src, dst, send, recv, peer):
         return pltpu.make_async_remote_copy(
@@ -88,6 +86,9 @@
             return 0
 
         lax.fori_loop(0, N, put, 0)
+    pl.semaphore_wait(barrier, len(peers))
+    for t, j in order:
+        px, py = (x + t) % N, (y + j) % N
         if j:
             at = (j - 1) * N + t
             copy = remote(
@@ -103,8 +104,7 @@
             copy.start()
             first_b[t, j] = copy
     sent += list(first_a.values()) + list(first_b.values())
-    load_a.wait()
-    load_b.wait()
+    load_g.wait()
 
     def line_a(t):
         px = (x + t) % N
@@ -113,7 +113,7 @@
         total = lown[px, y, :, 0:HALF, :].astype(jnp.float32)
         for j in range(1, N):
             total = total + r1a[j - 1, px].astype(jnp.float32)
-        return N * g_a[px] - total
+        return N * newp[px, y, :, 0:HALF, :] - total
 
     def line_b(j):
         py = (y + j) % N
@@ -122,7 +122,7 @@
         total = lown[x, py, :, HALF : 2 * HALF, :].astype(jnp.float32)
         for t in range(1, N):
             total = total + r1b[t - 1, py].astype(jnp.float32)
-        return N * g_b[py] - total
+        return N * newp[x, py, :, HALF : 2 * HALF, :] - total
 
     second = []
     for s in range(1, N):
@@ -251,6 +251,9 @@
     for k in range(N):
         xall[x, y, k] = mm(look[k], mults[k] * scales[k]).astype(jnp.bfloat16)
 
+    def use(px, py):
+        newp[px, py] = newp[px, py] - factor * xall[px, py].astype(jnp.float32)
+
     x_direct = gather_own(xall, x_send, x_recv)
     sent += x_direct
 
@@ -265,10 +268,17 @@
         fresh = decay_rate * old + (seen - LOOK_M * old) * (1.0 / LOOK_P)
         newmom[s] = jnp.where(used > 0, fresh, old)
 
+    use(x, y)
     x_forward = gather_forward(xall, x_direct, xf_send, xf_recv)
     sent += x_forward
-    for copy in x_forward:
-        copy.wait_recv()
+    for j in range(1, N):
+        use((x - j + N) % N, y)
+        use(x, (y - j + N) % N)
+    for a in range(1, N):
+        for b in range(1, N):
+            x_forward[((a - 1) * 2) * (N - 1) + b - 1].wait_recv()
+            x_forward[((b - 1) * 2 + 1) * (N - 1) + a - 1].wait_recv()
+            use((x - a + N) % N, (y - b + N) % N)
     for copy in sent:
         copy.wait_send()
 
@@ -291,13 +301,14 @@
     def in_hbm(array):
         return pltpu.with_memory_space_constraint(array, pltpu.HBM)
 
+    factor = math.sqrt(height * lax.axis_size("fsdp") / width)
     bf, f4 = jnp.bfloat16, jnp.float32
     dma = pltpu.SemaphoreType.DMA
     vmem = pltpu.VMEM
-    gathered, new_momentum = pl.pallas_call(
-        kernel,
+    new_params, new_momentum = pl.pallas_call(
+        functools.partial(kernel, factor),
         out_shape=(
-            jax.ShapeDtypeStruct((N, N, N, height, width), bf),
+            jax.ShapeDtypeStruct((N, N, N, height, width), f4),
             jax.ShapeDtypeStruct((slots, height, width), f4),
         ),
         in_specs=[
@@ -309,8 +320,7 @@
         out_specs=(pl.BlockSpec(memory_space=vmem), pl.BlockSpec(memory_space=vmem)),
         scratch_shapes=[
             vmem((N, N, N, height, width), bf),
-            vmem((N, N, HALF, width), f4),
-            vmem((N, N, HALF, width), f4),
+            vmem((N, N, N, height, width), bf),
             vmem((N - 1, N, N, HALF, width), bf),
             vmem((N - 1, N, N, HALF, width), bf),
             vmem((N - 1, N, HALF, width), bf),
@@ -326,7 +336,7 @@
             vmem((FAR - 1, HALF, width), bf),
             vmem((2 * N, HALF, width), bf),
             dma((N * N,)),
-            dma((2,)),
+            dma,
             dma((2, (N - 1) * N)),
             dma((2, (N - 1) * N)),
             dma((2, N - 1)),
@@ -356,9 +366,7 @@
         in_hbm(global_params.reshape(N, N, N, height, width)),
         momentum[0],
     )
-    factor = math.sqrt(height * lax.axis_size("fsdp") / width)
-    update = gathered.reshape(blocks, height, width).astype(f4)
-    return (global_params - factor * update, new_momentum[None])
+    return (new_params.reshape(blocks, height, width), new_momentum[None])
 
 
 def solution(mesh):

time: 98.3 us -> 95.4 us (0.970)
  other arithmetic: 5.18 us -> 1.8 us
    sub x1 -> x0, other arithmetic: 2.83 us -> none  [shards(): return (global_params - factor * update, new_momentum[None])]
    unnamed x5 -> x4, local copies, waits for them, and re-layouts: 3.38 us -> 3.77 us
where the time goes in v3:
time: 95.4 us; the launch traced here: 95.2 us
  Pallas kernels  89 us (93%)
  local copies, waits for them, and re-layouts  3.77 us (4%)
  other arithmetic  1.8 us (2%)
    pallas_call x1, Pallas kernels, shards(): pl.pallas_call(functools.partial(kernel, factor), out_shape=(jax.ShapeDty...  89 us
    unnamed x4, local copies, waits for them, and re-layouts  3.77 us

profile of v3, /device:TPU:1, one launch (start us, length us, event | category | flops | bytes accessed | tf_op | source)
XLA Modules:
  0.0 95.2 jit_solution(17778473985773074920)
XLA Ops:
  0.6 0.9 convert_reduce_fusion
  1.5 0.7 broadcast_select_fusion
  2.2 0.1 select_reduce_fusion
  2.4 0.1 pad_add_fusion.table
  2.4 0.0 copy-start
  2.4 1.0 %copy-done = f32[1,6,128,128]{3,2,1,0:T(8,128)S(1)} copy-done((f32[1,6,128,128]{3,2,1,0:T(8,128)S(1)}, f32[1,6,128,128]{3,2,1,0:T(8,128)}, u32[]{:S(2)}) %copy-start) | copy-done | bytes 393240
  3.5 89.0 %outer_step.1 = (f32[4,4,4,128,128]{4,3,2,1,0:T(8,128)S(1)}, f32[6,128,128]{2,1,0:T(8,128)S(1)}) custom-call(s32[144]{0:T(256)S(1)} %pad_add_fusion.table, bf16[4,4,4,128,128]{4,3,2,1,0:T(8,128)(2,1)} %bitcast.12, f32[4,4,4,128,128]{4,3,2,1,0:T(8,128)} %bitcast.11, f32[6,128,128]{2,1,0:T(8,128)S(1)} %bitcast.9), custom_call_target="tpu_custom_call" | custom-call | tf_op jit(solution)/shard_map/outer_step/pallas_call | solution.py:308
  92.5 2.0 %copy.8 = f32[64,128,128]{2,1,0:T(8,128)} copy(f32[64,128,128]{2,1,0:T(8,128)S(1)} %bitcast.8) | data formatting | bytes 8388608
  94.5 0.7 copy.9
  (1 shorter events, 0.0 us)
Async XLA Ops:
  2.4 1.0 %copy-start = (f32[1,6,128,128]{3,2,1,0:T(8,128)S(1)}, f32[1,6,128,128]{3,2,1,0:T(8,128)}, u32[]{:S(2)}) copy-start(f32[1,6,128,128]{3,2,1,0:T(8,128)} %param.6) | copy-start | bytes 1179652
